TPU v7x, 128 devices: a whole 4x4x4 slice. The times are simulated.
128 devices in a mesh: ctx: 16 (over y, x), head: 8 (over z, core).
Axes of the slice: x: 4, y: 4, z: 4, core: 2. Of those that a mesh axis runs over, the one named last changes fastest.
Arguments:
- query_input: bfloat16 [16, 1024, 4096], P('ctx', 'head'), may hold values from -6 to 6
- key_input: bfloat16 [16, 1024, 512], P('ctx', 'head'), may hold values from -6 to 6
- value_input: bfloat16 [16, 1024, 512], P('ctx', 'head'), may hold values from -6 to 6
- grad_input: bfloat16 [16, 1024, 4096], P('ctx', 'head'), may hold values from -6 to 6
Outputs:
- attended: bfloat16 [16, 1024, 4096], P('ctx', 'head')
- query_grad: float32 [16, 1024, 4096], P('ctx', 'head')
- key_grad: float32 [16, 1024, 512], P('ctx', 'head')
- value_grad: float32 [16, 1024, 512], P('ctx', 'head')
All inputs are finite; a program needn't handle non-finite values.
Results may differ from a plain program's by a relative error of at most 0.0076.
Values may be sent and summed in bfloat16 or wider, within the bound.
No kernel may reach another device: no remote copies, remote signals or barrier semaphores. Data moves between devices by JAX's collectives and lax.ppermute only.
A program may use at most 192 MiB of HBM per device.

v0:
```python
import math
import jax
import jax.numpy as jnp
from jax import lax
from jax.sharding import PartitionSpec as P

HD = 128


def from_partner(value, axis, apart):
    mask = 2**apart
    pairs = [(source, source ^ mask) for source in range(lax.axis_size(axis))]
    return lax.ppermute(value, axis, pairs)


def sent_together(arrays, axis, dim, along):
    both = jnp.concatenate(arrays, axis=along)
    filled, at, outs = (lax.all_gather(both, axis, axis=dim, tiled=True), 0, [])
    for a in arrays:
        outs.append(lax.slice_in_dim(filled, at, at + a.shape[along], axis=along))
        at += a.shape[along]
    return tuple(outs)


def attend(query_split, grad_split, query_pos, key_all, value_all, key_span, scaling):
    rows, pair_heads, sharing, head_dim = query_split.shape
    block_total = (jnp.max(query_pos) + key_span) // key_span

    def block_scores(begin_row):
        key_block = lax.dynamic_slice_in_dim(key_all, begin_row, key_span, 0).reshape(
            key_span, pair_heads, head_dim
        )
        raw_scores = (
            jnp.einsum("ihgd,jhd->hgij", query_split, key_block, preferred_element_type=jnp.float32)
            * scaling
        )
        allowed = (begin_row + jnp.arange(key_span, dtype=jnp.int32))[None, :] <= query_pos[:, None]
        return (jnp.where(allowed, raw_scores, -jnp.inf), key_block)

    def value_slice(begin_row):
        return lax.dynamic_slice_in_dim(value_all, begin_row, key_span, 0).reshape(
            key_span, pair_heads, head_dim
        )

    def stats_pass(step_num, state_in):
        running_max, running_sum = state_in
        scores, unused = block_scores(step_num * key_span)
        highest = jnp.maximum(running_max, jnp.max(scores, axis=-1))
        rescale = jnp.exp(running_max - highest)
        running_sum = running_sum * rescale + jnp.sum(jnp.exp(scores - highest[..., None]), axis=-1)
        return (highest, running_sum)

    stat_shape = (pair_heads, sharing, rows)
    highest, running_sum = lax.fori_loop(
        0,
        block_total,
        stats_pass,
        (jnp.full(stat_shape, -jnp.inf, jnp.float32), jnp.zeros(stat_shape, jnp.float32)),
    )
    log_total = highest + jnp.log(running_sum)

    def output_pass(step_num, running_out):
        begin_row = step_num * key_span
        scores, unused = block_scores(begin_row)
        weights = jnp.exp(scores - log_total[..., None]).astype(jnp.bfloat16)
        return running_out + jnp.einsum(
            "hgij,jhd->hgid", weights, value_slice(begin_row), preferred_element_type=jnp.float32
        )

    running_out = lax.fori_loop(
        0, block_total, output_pass, jnp.zeros(stat_shape + (head_dim,), jnp.float32)
    )
    attended = running_out.transpose(2, 0, 1, 3).astype(jnp.bfloat16)
    row_dot = jnp.sum(
        grad_split.astype(jnp.float32) * attended.astype(jnp.float32), axis=-1
    ).transpose(1, 2, 0)

    def grad_pass(step_num, state_in):
        begin_row = step_num * key_span
        scores, key_block = block_scores(begin_row)
        value_block = value_slice(begin_row)
        normalized = jnp.exp(scores - log_total[..., None])
        weights = normalized.astype(jnp.bfloat16)
        weight_grad = jnp.einsum(
            "ihgd,jhd->hgij", grad_split, value_block, preferred_element_type=jnp.float32
        )
        score_grad = (normalized * (weight_grad - row_dot[..., None])).astype(jnp.bfloat16)
        query_sum = state_in[0] + jnp.einsum(
            "hgij,jhd->ihgd", score_grad, key_block, preferred_element_type=jnp.float32
        )
        return (query_sum,)

    query_zero = jnp.zeros((rows, pair_heads, sharing, head_dim), jnp.float32)
    initial = (query_zero,)
    gradients = lax.fori_loop(0, block_total, grad_pass, initial)
    sums_out = None
    return (attended, gradients[0], sums_out, log_total, row_dot)


def on_device(query_input, key_input, value_input, grad_input):
    local_rows = query_input.shape[1]
    query_width = query_input.shape[2]
    pair_width = key_input.shape[2]
    pair_heads = pair_width // HD
    sharing = query_width // pair_width
    local_heads = pair_heads * sharing
    block_count = lax.axis_size("ctx")
    block_rows = 2 * local_rows
    all_rows = block_count * block_rows
    key_span = min(512, all_rows)
    scaling = 1.0 / math.sqrt(HD)
    block_index = lax.axis_index("ctx")
    half_index = lax.axis_index("head") % 2
    block_first = block_index * block_rows
    first_row = block_first + half_index * local_rows
    query_local = query_input.reshape(local_rows, query_width)
    grad_local = grad_input.reshape(local_rows, query_width)
    own_pairs = jnp.stack(
        [key_input.reshape(local_rows, pair_width), value_input.reshape(local_rows, pair_width)]
    )
    partner_pairs = from_partner(own_pairs, "head", 0)
    block_pairs = jnp.where(
        half_index == 0,
        jnp.concatenate([own_pairs, partner_pairs], axis=1),
        jnp.concatenate([partner_pairs, own_pairs], axis=1),
    )
    gathered_pairs = lax.all_gather(block_pairs, "ctx", axis=1, tiled=True)
    key_all = gathered_pairs[0]
    value_all = gathered_pairs[1]
    query_split = query_local.reshape(local_rows, pair_heads, sharing, HD)
    grad_split = grad_local.reshape(local_rows, pair_heads, sharing, HD)
    query_pos = first_row + jnp.arange(local_rows, dtype=jnp.int32)
    sums_in = None
    attended, query_sum, sums_out, log_total, row_dot = attend(
        query_split, grad_split, query_pos, key_all, value_all, key_span, scaling
    )
    query_grad = scaling * query_sum
    total_rows = log_total.reshape(local_heads, local_rows).T
    dot_rows = row_dot.reshape(local_heads, local_rows).T
    total_all, dot_all = sent_together((total_rows, dot_rows), "ctx", 0, 1)
    block_keys = block_pairs[0].reshape(block_rows, pair_heads, HD)
    block_values = block_pairs[1].reshape(block_rows, pair_heads, HD)
    key_pos = block_first + jnp.arange(block_rows, dtype=jnp.int32)
    zero_rows = jnp.zeros((block_rows, pair_width), jnp.float32)
    query_piece, grad_piece = sent_together((query_local, grad_local), "ctx", 0, 1)
    piece_rows = query_piece.shape[0]
    query_span = math.gcd(piece_rows, 512)
    span_total = piece_rows // query_span

    def one_block(step_num, sums_in):
        offset = step_num * query_span
        gathered_index = offset + jnp.arange(query_span, dtype=jnp.int32)
        row_pos = (
            gathered_index // local_rows * block_rows
            + half_index * local_rows
            + gathered_index % local_rows
        )

        def accumulate(sums_now):
            query_block = lax.dynamic_slice_in_dim(query_piece, offset, query_span, 0).reshape(
                query_span, pair_heads, sharing, HD
            )
            grad_block = lax.dynamic_slice_in_dim(grad_piece, offset, query_span, 0).reshape(
                query_span, pair_heads, sharing, HD
            )
            total_block = lax.dynamic_slice_in_dim(total_all, offset, query_span, 0).T.reshape(
                pair_heads, sharing, query_span
            )
            dot_block = lax.dynamic_slice_in_dim(dot_all, offset, query_span, 0).T.reshape(
                pair_heads, sharing, query_span
            )
            raw_scores = (
                jnp.einsum(
                    "ihgd,jhd->hgij", query_block, block_keys, preferred_element_type=jnp.float32
                )
                * scaling
            )
            allowed = key_pos[None, :] <= row_pos[:, None]
            normalized = jnp.exp(jnp.where(allowed, raw_scores, -jnp.inf) - total_block[..., None])
            weights = normalized.astype(jnp.bfloat16)
            weight_grad = jnp.einsum(
                "ihgd,jhd->hgij", grad_block, block_values, preferred_element_type=jnp.float32
            )
            score_grad = (normalized * (weight_grad - dot_block[..., None])).astype(jnp.bfloat16)
            key_add = jnp.einsum(
                "hgij,ihgd->jhd", score_grad, query_block, preferred_element_type=jnp.float32
            ).reshape(block_rows, pair_width)
            value_add = jnp.einsum(
                "hgij,ihgd->jhd", weights, grad_block, preferred_element_type=jnp.float32
            ).reshape(block_rows, pair_width)
            return (sums_now[0] + key_add, sums_now[1] + value_add)

        def unchanged(sums_now):
            return sums_now

        return lax.cond(jnp.max(row_pos) >= block_first, accumulate, unchanged, sums_in)

    key_sum, value_sum = lax.fori_loop(0, span_total, one_block, (zero_rows, zero_rows))
    outgoing = jnp.stack(
        [
            lax.dynamic_slice_in_dim(key_sum, (1 - half_index) * local_rows, local_rows, 0),
            lax.dynamic_slice_in_dim(value_sum, (1 - half_index) * local_rows, local_rows, 0),
        ]
    )
    incoming = from_partner(outgoing.astype(jnp.bfloat16), "head", 0).astype(outgoing.dtype)
    key_mine = (
        lax.dynamic_slice_in_dim(key_sum, half_index * local_rows, local_rows, 0) + incoming[0]
    )
    value_mine = (
        lax.dynamic_slice_in_dim(value_sum, half_index * local_rows, local_rows, 0) + incoming[1]
    )
    key_grad = scaling * key_mine
    return (
        attended.reshape(1, local_rows, query_width),
        query_grad.reshape(1, local_rows, query_width),
        key_grad.reshape(1, local_rows, pair_width),
        value_mine.reshape(1, local_rows, pair_width),
    )


def solution(mesh):
    in_specs = (
        P("ctx", "head", None),
        P("ctx", "head", None),
        P("ctx", "head", None),
        P("ctx", "head", None),
    )
    out_specs = (
        P("ctx", "head", None),
        P("ctx", "head", None),
        P("ctx", "head", None),
        P("ctx", "head", None),
    )
    return jax.shard_map(
        on_device, mesh=mesh, in_specs=in_specs, out_specs=out_specs, check_vma=False
    )
```

profile of v0, /device:TPU:1, one launch (start us, length us, event | category | flops | bytes accessed | tf_op | source)
XLA Modules:
  0.0 464.3 jit_solution(15359233953880189449)
XLA Ops:
  23.0 62.7 %all-gather.3.cloned.1.call-done = bf16[2,4096,512]{2,1,0:T(8,128)(2,1)} async-done(((bf16[2,256,512]{2,1,0:T(8,128)(2,1)}), bf16[2,4096,512]{2,1,0:T(8,128)(2,1)}) %all-gather.3.cloned.1.call-update) | async-done | bytes 8388624 | tf_op jit(solution)/shard_map/all_gather | solution.py:127
  85.7 5.7 %slice_bitcast_fusion = (bf16[4096,512]{1,0:T(8,128)(2,1)}, bf16[4096,512]{1,0:T(8,128)(2,1)}) fusion(bf16[2,4096,512]{2,1,0:T(8,128)(2,1)} %all-gather.3.cloned.1.call-done), kind=kLoop, calls=%fused_computation.84 | loop fusion | bytes 16777216 | tf_op jit(solution)/shard_map/squeeze | solution.py:129
  91.4 6.4 %copy.72 = bf16[4096,512]{0,1:T(8,128)(2,1)} copy(bf16[4096,512]{1,0:T(8,128)(2,1)} %get-tuple-element.831) | data formatting | bytes 8388608
  97.8 6.7 %copy.74 = bf16[4096,512]{0,1:T(8,128)(2,1)} copy(bf16[4096,512]{1,0:T(8,128)(2,1)} %get-tuple-element.830) | data formatting | bytes 8388608
  110.7 7.7 %while.55 = (s32[]{:T(128)}, f32[4,8,128,128]{3,2,1,0:T(8,128)}, s32[]{:T(128)}, bf16[4096,512]{0,1:T(8,128)(2,1)}, bf16[128,4,8,128]{3,0,2,1:T(8,128)(2,1)S(1)}...) while((s32[]{:T(128)}, f32[4,8,128,128]{3,2,1,0:T(8,128)}, ...), condition=%wide.region_6.7_spmd.clone, body=%wide.region_5.6_spmd.clone.sunk | while | flops 1082720896 | bytes 8541367 | solution.py:70
  112.1 6.2 %fusion.108 = f32[4,8,128,128]{3,2,1,0:T(8,128)} fusion(f32[4,8,128,128]{3,2,1,0:T(8,128)} %get-tuple-element.1133, bf16[512,4,128,1]{0,2,3,1:T(8,128)(2,1)S(1)} %bitcast.231, f32[4,8,128]{2,1,0:T(8,128)S(1)} %get-tuple-element.1149, pred[128,512]{0,1:T(8,128)(4,1)S(1)} %broadcast_compare_fusion.8, bf16[512,4,128,1]{0,2,3,1:T(8,128)(2,1)S(1)} %bitcast.232, ...), kind=kOutput, calls=%fused_computation.46.clone.1 | convolution fusion | flops 1082654720 | bytes 6373376 | tf_op jit(solution)/shard_map/while/body/hgij,jhd->hgid/dot_general | solution.py:66
  122.2 109.7 %all_gather.11 = f32[2048,64]{0,1:T(8,128)S(1)} all-gather(f32[128,64]{0,1:T(8,128)S(1)} %pad_maximum_fusion.2), channel_id=1, replica_groups=mesh['ctx'=16,'head'=8] {'ctx'}, dimensions={0}, use_global_device_ids=true | all-gather | bytes 557056 | tf_op jit(solution)/shard_map/all_gather | solution.py:18
  234.3 14.4 %while.56 = (s32[]{:T(128)}, f32[128,4,8,128]{0,3,2,1:T(8,128)}, s32[]{:T(128)}, bf16[4096,512]{0,1:T(8,128)(2,1)}, bf16[128,4,8,128]{3,0,2,1:T(8,128)(2,1)S(1)}...) while((s32[]{:T(128)}, f32[128,4,8,128]{0,3,2,1:T(8,128)}, ...), condition=%wide.region_9.10_spmd.clone, body=%wide.region_8.9_spmd.clone.sunk | while | flops 1623786112 | bytes 31102180 | solution.py:95
  240.3 8.3 %bitcast_add_fusion.4 = f32[128,4,8,128]{0,3,2,1:T(8,128)} fusion(f32[128,4,8,128]{0,3,2,1:T(8,128)} %get-tuple-element.1171, bf16[512,4,128,1]{0,2,3,1:T(8,128)(2,1)S(1)} %bitcast.225, f32[4,512,128,8]{2,1,3,0:T(8,128)} %fusion.115, f32[4,8,128]{2,1,0:T(8,128)S(1)} %get-tuple-element.1192, f32[4,8,128]{2,1,0:T(8,128)S(1)} %get-tuple-element.1189, ...), kind=kOutput, calls=%fused_computation.63.clone.1 | convolution fusion | flops 1086849024 | bytes 14778368 | tf_op jit(solution)/shard_map/while/body/hgij,jhd->ihgd/dot_general | solution.py:88
  248.7 48.5 %all-gather.5.cloned.1.call-done = bf16[2048,8192]{0,1:T(8,128)(2,1)} async-done(((bf16[128,8192]{0,1:T(8,128)(2,1)}), bf16[2048,8192]{0,1:T(8,128)(2,1)}) %all-gather.5.cloned.1.call-update) | async-done | bytes 33554448 | tf_op jit(solution)/shard_map/all_gather | solution.py:18
  297.2 23.5 %fusion.67 = (bf16[2048,4096]{0,1:T(8,128)(2,1)}, bf16[2048,4096]{0,1:T(8,128)(2,1)}) fusion(bf16[2048,8192]{0,1:T(8,128)(2,1)} %all-gather.5.cloned.1.call-done), kind=kLoop, calls=%fused_computation.107 | loop fusion | bytes 67108864 | tf_op jit(solution)/shard_map/slice | solution.py:20
  320.7 129.3 %while.57 = (s32[]{:T(128)}, f32[256,512]{0,1:T(8,128)S(1)}, f32[256,512]{0,1:T(8,128)S(1)}, s32[]{:T(128)}, s32[]{:T(128)}, /*index=5*/bf16[2048,4096]{0,1:T(8,...) while((s32[]{:T(128)}, f32[256,512]{0,1:T(8,128)S(1)}, ...), condition=%wide.region_14.15_spmd.clone.clone, body=%wide.region_10.14_spmd.clone.clone.sunk | while | flops 4337315840 | bytes 174399952 | solution.py:198
  322.0 31.0 %conditional.4 = ((f32[256,512]{0,1:T(8,128)S(1)}, f32[256,512]{0,1:T(8,128)S(1)})) conditional(s32[]{:T(128)} %convert_element_type.67, (f32[256,512]{0,1:T(8,128)S(1)}, f32[256,512]{0,1:T(8,128)S(1)}) %tuple.142, (s32[]{:T(128)}, bf16[2048,4096]{0,1:T(8,128)(2,1)}, s32[]{:T(128)}, s32[512]{0:T(512)S(1)}, bf16[256,4,128]{2,0,1:T(8,128)(2,1)S(1)}, ...), branch_computations={%region_12.12_spmd, %region_13.13_spmd} | conditional | flops 4337303552 | bytes 174396576 | solution.py:196
  332.4 7.7 %fusion.12 = f32[4,128,256,1]{2,1,3,0:T(8,128)S(1)} fusion(bf16[512,4,8,128]{0,3,2,1:T(8,128)(2,1)} %bitcast.222, f32[4,512,8,256]{3,1,2,0:T(8,128)S(1)} %fusion.18, f32[4,8,512]{2,1,0:T(8,128)S(1)} %dynamic-slice_bitcast_fusion.1, pred[512,256]{1,0:T(8,128)(4,1)S(1)} %broadcast_compare_fusion), kind=kOutput, calls=%fused_computation.10 | convolution fusion | flops 1090519040 | bytes 21692416 | tf_op jit(solution)/shard_map/while/body/eval_jaxpr/cond/branch_1_fun/hgij,ihgd->jhd/dot_general | solution.py:188
  341.0 11.8 %fusion.15 = f32[4,128,256,1]{2,1,3,0:T(8,128)S(1)} fusion(bf16[512,4,8,128]{0,3,2,1:T(8,128)(2,1)} %bitcast.221, f32[4,512,8,256]{3,1,2,0:T(8,128)} %copy-done, bf16[512,4,8,128]{0,3,2,1:T(8,128)(2,1)} %bitcast.223, f32[4,8,512]{2,1,0:T(8,128)S(1)} %dynamic-slice_bitcast_fusion, f32[4,8,512]{2,1,0:T(8,128)S(1)} %dynamic-slice_bitcast_fusion.1, ...), kind=kOutput, calls=%fused_computation.12 | convolution fusion | flops 2172649472 | bytes 26214400 | tf_op jit(solution)/shard_map/while/body/eval_jaxpr/cond/branch_1_fun/hgij,ihgd->jhd/dot_general | solution.py:185
  354.4 31.0 %conditional.4 = ((f32[256,512]{0,1:T(8,128)S(1)}, f32[256,512]{0,1:T(8,128)S(1)})) conditional(s32[]{:T(128)} %convert_element_type.67, (f32[256,512]{0,1:T(8,128)S(1)}, f32[256,512]{0,1:T(8,128)S(1)}) %tuple.142, (s32[]{:T(128)}, bf16[2048,4096]{0,1:T(8,128)(2,1)}, s32[]{:T(128)}, s32[512]{0:T(512)S(1)}, bf16[256,4,128]{2,0,1:T(8,128)(2,1)S(1)}, ...), branch_computations={%region_12.12_spmd, %region_13.13_spmd} | conditional | flops 4337303552 | bytes 174396576 | solution.py:196
  364.8 7.7 %fusion.12 = f32[4,128,256,1]{2,1,3,0:T(8,128)S(1)} fusion(bf16[512,4,8,128]{0,3,2,1:T(8,128)(2,1)} %bitcast.222, f32[4,512,8,256]{3,1,2,0:T(8,128)S(1)} %fusion.18, f32[4,8,512]{2,1,0:T(8,128)S(1)} %dynamic-slice_bitcast_fusion.1, pred[512,256]{1,0:T(8,128)(4,1)S(1)} %broadcast_compare_fusion), kind=kOutput, calls=%fused_computation.10 | convolution fusion | flops 1090519040 | bytes 21692416 | tf_op jit(solution)/shard_map/while/body/eval_jaxpr/cond/branch_1_fun/hgij,ihgd->jhd/dot_general | solution.py:188
  373.4 11.8 %fusion.15 = f32[4,128,256,1]{2,1,3,0:T(8,128)S(1)} fusion(bf16[512,4,8,128]{0,3,2,1:T(8,128)(2,1)} %bitcast.221, f32[4,512,8,256]{3,1,2,0:T(8,128)} %copy-done, bf16[512,4,8,128]{0,3,2,1:T(8,128)(2,1)} %bitcast.223, f32[4,8,512]{2,1,0:T(8,128)S(1)} %dynamic-slice_bitcast_fusion, f32[4,8,512]{2,1,0:T(8,128)S(1)} %dynamic-slice_bitcast_fusion.1, ...), kind=kOutput, calls=%fused_computation.12 | convolution fusion | flops 2172649472 | bytes 26214400 | tf_op jit(solution)/shard_map/while/body/eval_jaxpr/cond/branch_1_fun/hgij,ihgd->jhd/dot_general | solution.py:185
  386.7 31.0 %conditional.4 = ((f32[256,512]{0,1:T(8,128)S(1)}, f32[256,512]{0,1:T(8,128)S(1)})) conditional(s32[]{:T(128)} %convert_element_type.67, (f32[256,512]{0,1:T(8,128)S(1)}, f32[256,512]{0,1:T(8,128)S(1)}) %tuple.142, (s32[]{:T(128)}, bf16[2048,4096]{0,1:T(8,128)(2,1)}, s32[]{:T(128)}, s32[512]{0:T(512)S(1)}, bf16[256,4,128]{2,0,1:T(8,128)(2,1)S(1)}, ...), branch_computations={%region_12.12_spmd, %region_13.13_spmd} | conditional | flops 4337303552 | bytes 174396576 | solution.py:196
  397.1 7.7 %fusion.12 = f32[4,128,256,1]{2,1,3,0:T(8,128)S(1)} fusion(bf16[512,4,8,128]{0,3,2,1:T(8,128)(2,1)} %bitcast.222, f32[4,512,8,256]{3,1,2,0:T(8,128)S(1)} %fusion.18, f32[4,8,512]{2,1,0:T(8,128)S(1)} %dynamic-slice_bitcast_fusion.1, pred[512,256]{1,0:T(8,128)(4,1)S(1)} %broadcast_compare_fusion), kind=kOutput, calls=%fused_computation.10 | convolution fusion | flops 1090519040 | bytes 21692416 | tf_op jit(solution)/shard_map/while/body/eval_jaxpr/cond/branch_1_fun/hgij,ihgd->jhd/dot_general | solution.py:188
  405.7 11.8 %fusion.15 = f32[4,128,256,1]{2,1,3,0:T(8,128)S(1)} fusion(bf16[512,4,8,128]{0,3,2,1:T(8,128)(2,1)} %bitcast.221, f32[4,512,8,256]{3,1,2,0:T(8,128)} %copy-done, bf16[512,4,8,128]{0,3,2,1:T(8,128)(2,1)} %bitcast.223, f32[4,8,512]{2,1,0:T(8,128)S(1)} %dynamic-slice_bitcast_fusion, f32[4,8,512]{2,1,0:T(8,128)S(1)} %dynamic-slice_bitcast_fusion.1, ...), kind=kOutput, calls=%fused_computation.12 | convolution fusion | flops 2172649472 | bytes 26214400 | tf_op jit(solution)/shard_map/while/body/eval_jaxpr/cond/branch_1_fun/hgij,ihgd->jhd/dot_general | solution.py:185
  419.0 31.0 %conditional.4 = ((f32[256,512]{0,1:T(8,128)S(1)}, f32[256,512]{0,1:T(8,128)S(1)})) conditional(s32[]{:T(128)} %convert_element_type.67, (f32[256,512]{0,1:T(8,128)S(1)}, f32[256,512]{0,1:T(8,128)S(1)}) %tuple.142, (s32[]{:T(128)}, bf16[2048,4096]{0,1:T(8,128)(2,1)}, s32[]{:T(128)}, s32[512]{0:T(512)S(1)}, bf16[256,4,128]{2,0,1:T(8,128)(2,1)S(1)}, ...), branch_computations={%region_12.12_spmd, %region_13.13_spmd} | conditional | flops 4337303552 | bytes 174396576 | solution.py:196
  429.4 7.7 %fusion.12 = f32[4,128,256,1]{2,1,3,0:T(8,128)S(1)} fusion(bf16[512,4,8,128]{0,3,2,1:T(8,128)(2,1)} %bitcast.222, f32[4,512,8,256]{3,1,2,0:T(8,128)S(1)} %fusion.18, f32[4,8,512]{2,1,0:T(8,128)S(1)} %dynamic-slice_bitcast_fusion.1, pred[512,256]{1,0:T(8,128)(4,1)S(1)} %broadcast_compare_fusion), kind=kOutput, calls=%fused_computation.10 | convolution fusion | flops 1090519040 | bytes 21692416 | tf_op jit(solution)/shard_map/while/body/eval_jaxpr/cond/branch_1_fun/hgij,ihgd->jhd/dot_general | solution.py:188
  438.0 11.8 %fusion.15 = f32[4,128,256,1]{2,1,3,0:T(8,128)S(1)} fusion(bf16[512,4,8,128]{0,3,2,1:T(8,128)(2,1)} %bitcast.221, f32[4,512,8,256]{3,1,2,0:T(8,128)} %copy-done, bf16[512,4,8,128]{0,3,2,1:T(8,128)(2,1)} %bitcast.223, f32[4,8,512]{2,1,0:T(8,128)S(1)} %dynamic-slice_bitcast_fusion, f32[4,8,512]{2,1,0:T(8,128)S(1)} %dynamic-slice_bitcast_fusion.1, ...), kind=kOutput, calls=%fused_computation.12 | convolution fusion | flops 2172649472 | bytes 26214400 | tf_op jit(solution)/shard_map/while/body/eval_jaxpr/cond/branch_1_fun/hgij,ihgd->jhd/dot_general | solution.py:185
  (133 shorter events, 95.0 us)
Async XLA Ops:
  7.2 78.5 %all-gather.3.cloned.1.call-start = ((), (), s32[]{:S(2)}) async-start(), calls=%async_computation | async-start | bytes 8912896 | tf_op jit(solution)/shard_map/all_gather | solution.py:127
  9.0 2.7 collective-permute-start
  12.7 284.4 %all-gather.5.cloned.1.call-start = ((), (), s32[]{:S(2)}) async-start(), calls=%async_computation.1 | async-start | bytes 35651584 | tf_op jit(solution)/shard_map/all_gather | solution.py:18
  234.3 6.0 %copy-start.4 = (bf16[128,4,8,128]{3,0,2,1:T(8,128)(2,1)S(1)}, bf16[128,4,8,128]{3,0,2,1:T(8,128)(2,1)}, u32[]{:S(2)}) copy-start(bf16[128,4,8,128]{3,0,2,1:T(8,128)(2,1)} %get-tuple-element.1191) | copy-start | bytes 3145732 | tf_op jit(solution)/shard_map/while
  328.9 2.4 copy-start.1
  331.4 8.8 %copy-start = (f32[4,512,8,256]{3,1,2,0:T(8,128)}, f32[4,512,8,256]{3,1,2,0:T(8,128)S(1)}, u32[]{:S(2)}) copy-start(f32[4,512,8,256]{3,1,2,0:T(8,128)S(1)} %fusion.18) | copy-start | bytes 50331652 | tf_op jit(solution)/shard_map/while/body/eval_jaxpr/cond
  332.4 8.6 %copy-start.5 = (bf16[256,4,128]{2,0,1:T(8,128)(2,1)S(1)}, bf16[256,4,128]{2,0,1:T(8,128)(2,1)}, u32[]{:S(2)}) copy-start(bf16[256,4,128]{2,0,1:T(8,128)(2,1)} %get-tuple-element.452) | copy-start | bytes 786436 | tf_op jit(solution)/shard_map/while/body/eval_jaxpr/cond
  361.3 2.4 copy-start.1
  363.7 8.8 %copy-start = (f32[4,512,8,256]{3,1,2,0:T(8,128)}, f32[4,512,8,256]{3,1,2,0:T(8,128)S(1)}, u32[]{:S(2)}) copy-start(f32[4,512,8,256]{3,1,2,0:T(8,128)S(1)} %fusion.18) | copy-start | bytes 50331652 | tf_op jit(solution)/shard_map/while/body/eval_jaxpr/cond
  364.8 8.6 %copy-start.5 = (bf16[256,4,128]{2,0,1:T(8,128)(2,1)S(1)}, bf16[256,4,128]{2,0,1:T(8,128)(2,1)}, u32[]{:S(2)}) copy-start(bf16[256,4,128]{2,0,1:T(8,128)(2,1)} %get-tuple-element.452) | copy-start | bytes 786436 | tf_op jit(solution)/shard_map/while/body/eval_jaxpr/cond
  393.6 2.4 copy-start.1
  396.0 8.8 %copy-start = (f32[4,512,8,256]{3,1,2,0:T(8,128)}, f32[4,512,8,256]{3,1,2,0:T(8,128)S(1)}, u32[]{:S(2)}) copy-start(f32[4,512,8,256]{3,1,2,0:T(8,128)S(1)} %fusion.18) | copy-start | bytes 50331652 | tf_op jit(solution)/shard_map/while/body/eval_jaxpr/cond
  397.1 8.6 %copy-start.5 = (bf16[256,4,128]{2,0,1:T(8,128)(2,1)S(1)}, bf16[256,4,128]{2,0,1:T(8,128)(2,1)}, u32[]{:S(2)}) copy-start(bf16[256,4,128]{2,0,1:T(8,128)(2,1)} %get-tuple-element.452) | copy-start | bytes 786436 | tf_op jit(solution)/shard_map/while/body/eval_jaxpr/cond
  425.9 2.4 copy-start.1
  428.3 8.8 %copy-start = (f32[4,512,8,256]{3,1,2,0:T(8,128)}, f32[4,512,8,256]{3,1,2,0:T(8,128)S(1)}, u32[]{:S(2)}) copy-start(f32[4,512,8,256]{3,1,2,0:T(8,128)S(1)} %fusion.18) | copy-start | bytes 50331652 | tf_op jit(solution)/shard_map/while/body/eval_jaxpr/cond
  429.4 8.6 %copy-start.5 = (bf16[256,4,128]{2,0,1:T(8,128)(2,1)S(1)}, bf16[256,4,128]{2,0,1:T(8,128)(2,1)}, u32[]{:S(2)}) copy-start(bf16[256,4,128]{2,0,1:T(8,128)(2,1)} %get-tuple-element.452) | copy-start | bytes 786436 | tf_op jit(solution)/shard_map/while/body/eval_jaxpr/cond
  450.4 2.4 copy-start.2
  451.3 5.2 %collective-permute-start.1 = (bf16[2,128,512]{2,1,0:T(8,128)(2,1)}, bf16[2,128,512]{2,1,0:T(8,128)(2,1)S(1)}, u32[]{:S(2)}, u32[]{:S(2)}) collective-permute-start(bf16[2,128,512]{2,1,0:T(8,128)(2,1)} %pad_maximum_fusion.1), channel_id=1, source_target_pairs={{0,1},{1,0},{2,3},{3,2},{4,5},{5,4},{6,7},{7,6},{8,9},{9,8},{10,11... | collective-permute-start | bytes 786440 | tf_op jit(solution)/shard_map/ppermute | solution.py:13
  452.9 3.7 copy-start.3
Sparse Core Ops, SparseCore 0:
  12.9 72.7 all-gather.2
  87.8 209.3 all-gather.4
where the time goes:
time: 466 us; the launch traced here: 464 us
  waiting for transfers between devices  112 us (24%)
  blocking collectives  110 us (24%)
  matrix products  108 us (23%)
  local copies, waits for them, and re-layouts  99.7 us (21%)
  between operations  14.9 us (3%)
  other arithmetic  13.3 us (3%)
    all_gather x1, blocking collectives, sent_together(): filled, at, outs = (lax.all_gather(both, axis, axis=dim, tiled=True), 0, [])  110 us
    all_gather x1, waiting for transfers between devices, on_device(): gathered_pairs = lax.all_gather(block_pairs, 'ctx', axis=1, tiled=True)  62.7 us
    all_gather x1, waiting for transfers between devices, sent_together(): filled, at, outs = (lax.all_gather(both, axis, axis=dim, tiled=True), 0, [])  48.5 us
    dot_general x4, matrix products, accumulate(): jnp.einsum('hgij,ihgd->jhd', score_grad, query_block, preferred_element_t...  47.2 us
    dot_general x4, matrix products, accumulate(): jnp.einsum('hgij,ihgd->jhd', weights, grad_block, preferred_element_type=...  30.9 us
    slice x2, local copies, waits for them, and re-layouts, sent_together(): outs.append(lax.slice_in_dim(filled, at, at + a.shape[along], axis=along))  24.3 us
    unnamed x16, local copies, waits for them, and re-layouts  21.7 us
    dynamic_slice x4, local copies, waits for them, and re-layouts, accumulate(): lax.dynamic_slice_in_dim(grad_piece, offset, query_span, 0)  17.7 us
  transfers between devices with their start and end apart: 4, of which 3 were waited for; matrix products, arithmetic and copies ran while one was open for 14% of the time, Pallas kernels for 0%

commit v1 on v0

--- a/solution.py
+++ b/solution.py
@@ -124,7 +124,9 @@
         jnp.concatenate([own_pairs, partner_pairs], axis=1),
         jnp.concatenate([partner_pairs, own_pairs], axis=1),
     )
-    gathered_pairs = lax.all_gather(block_pairs, "ctx", axis=1, tiled=True)
+    gathered_pairs = jnp.concatenate(
+        lax.all_to_all(jnp.stack([block_pairs] * lax.axis_size("ctx")), "ctx", 0, 0), axis=1
+    )
     key_all = gathered_pairs[0]
     value_all = gathered_pairs[1]
     query_split = query_local.reshape(local_rows, pair_heads, sharing, HD)

time: 466 us -> 538 us (1.15)
  the two profiles are of different devices: /device:TPU:1 before, /device:TPU:71 now
where the time goes in v1:
time: 538 us; the launch traced here: 536 us
  matrix products  158 us (29%)
  waiting for transfers between devices  133 us (25%)
  local copies, waits for them, and re-layouts  104 us (19%)
  blocking collectives  96.4 us (18%)
  between operations  14.9 us (3%)
  other arithmetic  14.8 us (3%)
  starting transfers between devices  11.7 us (2%)
    all_to_all x1, waiting for transfers between devices, on_device(): lax.all_to_all(jnp.stack([block_pairs] * lax.axis_size('ctx')), 'ctx', 0, 0)  132 us
    all_gather x1, blocking collectives, sent_together(): filled, at, outs = (lax.all_gather(both, axis, axis=dim, tiled=True), 0, [])  96.4 us
    dot_general x4, matrix products, accumulate(): jnp.einsum('hgij,ihgd->jhd', score_grad, query_block, preferred_element_t...  47.1 us
    dot_general x4, matrix products, accumulate(): jnp.einsum('hgij,ihgd->jhd', weights, grad_block, preferred_element_type=...  36.2 us
    dot_general x4, matrix products, accumulate(): jnp.einsum('ihgd,jhd->hgij', query_block, block_keys, preferred_element_t...  32.5 us
    dynamic_slice x4, local copies, waits for them, and re-layouts, accumulate(): lax.dynamic_slice_in_dim(grad_piece, offset, query_span, 0)  23.7 us
    slice x2, local copies, waits for them, and re-layouts, sent_together(): outs.append(lax.slice_in_dim(filled, at, at + a.shape[along], axis=along))  23.5 us
    unnamed x21, local copies, waits for them, and re-layouts  21 us
  transfers between devices with their start and end apart: 4, of which 2 were waited for; matrix products, arithmetic and copies ran while one was open for 17% of the time, Pallas kernels for 0%

profile of v1, /device:TPU:71, one launch (start us, length us, event | category | flops | bytes accessed | tf_op | source)
XLA Modules:
  0.0 535.8 jit_solution(14777611810489807151)
XLA Ops:
  31.1 131.9 %all-to-all-done = bf16[16,2,256,512]{3,2,1,0:T(8,128)(2,1)} async-done(((bf16[16,2,256,512]{3,2,1,0:T(8,128)(2,1)}), bf16[16,2,256,512]{3,2,1,0:T(8,128)(2,1)}, u32[]{:S(2)}, u32[]{:S(2)}) %all-to-all-start) | async-done | bytes 8388640 | tf_op jit(solution)/shard_map/all_to_all | solution.py:128
  181.8 9.2 %while.54 = (s32[]{:T(128)}, f32[4,8,128]{2,1,0:T(8,128)S(1)}, f32[4,8,128]{2,1,0:T(8,128)S(1)}, s32[]{:T(128)}, bf16[4096,512]{0,1:T(8,128)(2,1)}, /*index=5*/b...) while((s32[]{:T(128)}, f32[4,8,128]{2,1,0:T(8,128)S(1)}, ...), condition=%wide.region_4.5_spmd.clone, body=%wide.region_1.4_spmd.clone.sunk | while | flops 551625344 | bytes 19813544 | solution.py:54
  192.6 15.4 %while.55 = (s32[]{:T(128)}, f32[4,8,128,128]{3,2,1,0:T(8,128)}, s32[]{:T(128)}, bf16[4096,512]{0,1:T(8,128)(2,1)}, bf16[128,4,8,128]{3,0,2,1:T(8,128)(2,1)S(1)}...) while((s32[]{:T(128)}, f32[4,8,128,128]{3,2,1,0:T(8,128)}, ...), condition=%wide.region_6.7_spmd.clone, body=%wide.region_5.6_spmd.clone.sunk | while | flops 1082720896 | bytes 8541359 | solution.py:70
  211.8 96.4 %all_gather.7 = f32[2048,64]{0,1:T(8,128)S(1)} all-gather(f32[128,64]{0,1:T(8,128)S(1)} %pad_maximum_fusion.3), channel_id=1, replica_groups=mesh['ctx'=16,'head'=8] {'ctx'}, dimensions={0}, use_global_device_ids=true | all-gather | bytes 557056 | tf_op jit(solution)/shard_map/all_gather | solution.py:18
  309.8 29.1 %while.56 = (s32[]{:T(128)}, f32[128,4,8,128]{0,3,2,1:T(8,128)}, s32[]{:T(128)}, bf16[4096,512]{0,1:T(8,128)(2,1)}, bf16[128,4,8,128]{3,0,2,1:T(8,128)(2,1)S(1)}...) while((s32[]{:T(128)}, f32[128,4,8,128]{0,3,2,1:T(8,128)}, ...), condition=%wide.region_9.10_spmd.clone, body=%wide.region_8.9_spmd.clone.sunk | while | flops 1623786112 | bytes 26907840 | solution.py:95
  315.7 8.6 %bitcast_add_fusion.4 = f32[128,4,8,128]{0,3,2,1:T(8,128)} fusion(f32[128,4,8,128]{0,3,2,1:T(8,128)} %get-tuple-element.1161, bf16[512,4,128,1]{0,2,3,1:T(8,128)(2,1)S(1)} %bitcast.225, f32[4,512,128,8]{2,1,3,0:T(8,128)} %fusion.116, f32[4,8,128]{2,1,0:T(8,128)S(1)} %get-tuple-element.1182, f32[4,8,128]{2,1,0:T(8,128)S(1)} %get-tuple-element.1179, ...), kind=kOutput, calls=%fused_computation.63.clone.1 | convolution fusion | flops 1086849024 | bytes 14778368 | tf_op jit(solution)/shard_map/while/body/hgij,jhd->ihgd/dot_general | solution.py:88
  330.3 8.6 %bitcast_add_fusion.4 = f32[128,4,8,128]{0,3,2,1:T(8,128)} fusion(f32[128,4,8,128]{0,3,2,1:T(8,128)} %get-tuple-element.1161, bf16[512,4,128,1]{0,2,3,1:T(8,128)(2,1)S(1)} %bitcast.225, f32[4,512,128,8]{2,1,3,0:T(8,128)} %fusion.116, f32[4,8,128]{2,1,0:T(8,128)S(1)} %get-tuple-element.1182, f32[4,8,128]{2,1,0:T(8,128)S(1)} %get-tuple-element.1179, ...), kind=kOutput, calls=%fused_computation.63.clone.1 | convolution fusion | flops 1086849024 | bytes 14778368 | tf_op jit(solution)/shard_map/while/body/hgij,jhd->ihgd/dot_general | solution.py:88
  338.9 23.5 %fusion.67 = (bf16[2048,4096]{0,1:T(8,128)(2,1)}, bf16[2048,4096]{0,1:T(8,128)(2,1)}) fusion(bf16[2048,8192]{0,1:T(8,128)(2,1)} %all-gather.2.cloned.1.call-done), kind=kLoop, calls=%fused_computation.104 | loop fusion | bytes 67108864 | tf_op jit(solution)/shard_map/slice | solution.py:20
  362.5 156.7 %while.57 = (s32[]{:T(128)}, f32[256,512]{0,1:T(8,128)S(1)}, f32[256,512]{0,1:T(8,128)S(1)}, s32[]{:T(128)}, s32[]{:T(128)}, /*index=5*/bf16[2048,4096]{0,1:T(8,...) while((s32[]{:T(128)}, f32[256,512]{0,1:T(8,128)S(1)}, ...), condition=%wide.region_14.15_spmd.clone.clone, body=%wide.region_10.14_spmd.clone.clone.sunk | while | flops 4337315840 | bytes 106242424 | solution.py:200
  363.9 37.8 %conditional.4 = ((f32[256,512]{0,1:T(8,128)S(1)}, f32[256,512]{0,1:T(8,128)S(1)})) conditional(s32[]{:T(128)} %convert_element_type.67, (f32[256,512]{0,1:T(8,128)S(1)}, f32[256,512]{0,1:T(8,128)S(1)}) %tuple.141, (s32[]{:T(128)}, bf16[2048,4096]{0,1:T(8,128)(2,1)}, s32[]{:T(128)}, s32[512]{0:T(512)S(1)}, bf16[256,4,128]{2,0,1:T(8,128)(2,1)S(1)}, ...), branch_computations={%region_12.12_spmd, %region_13.13_spmd} | conditional | flops 4337303552 | bytes 106239080 | solution.py:198
  372.5 8.1 %fusion.18 = f32[4,512,8,256]{3,1,2,0:T(8,128)} fusion(bf16[512,4,8,128]{0,3,2,1:T(8,128)(2,1)S(1)} %bitcast.220, bf16[256,4,128]{2,0,1:T(8,128)(2,1)S(1)} %get-tuple-element.449), kind=kOutput, calls=%fused_computation.16 | convolution fusion | flops 1073741824 | bytes 21233664 | tf_op jit(solution)/shard_map/while/body/eval_jaxpr/cond/branch_1_fun/ihgd,jhd->hgij/dot_general | solution.py:175
  380.7 11.8 %fusion.15 = f32[4,128,256,1]{2,1,3,0:T(8,128)S(1)} fusion(bf16[512,4,8,128]{0,3,2,1:T(8,128)(2,1)} %bitcast.221, f32[4,512,8,256]{3,1,2,0:T(8,128)} %fusion.18, bf16[512,4,8,128]{0,3,2,1:T(8,128)(2,1)} %bitcast.222, f32[4,8,512]{2,1,0:T(8,128)S(1)} %dynamic-slice_bitcast_fusion, f32[4,8,512]{2,1,0:T(8,128)S(1)} %dynamic-slice_bitcast_fusion.1, ...), kind=kOutput, calls=%fused_computation.12 | convolution fusion | flops 2172649472 | bytes 26214400 | tf_op jit(solution)/shard_map/while/body/eval_jaxpr/cond/branch_1_fun/hgij,ihgd->jhd/dot_general | solution.py:187
  392.4 9.1 %fusion.12 = f32[4,128,256,1]{2,1,3,0:T(8,128)S(1)} fusion(bf16[512,4,8,128]{0,3,2,1:T(8,128)(2,1)} %bitcast.223, f32[4,512,8,256]{3,1,2,0:T(8,128)} %fusion.18, f32[4,8,512]{2,1,0:T(8,128)S(1)} %dynamic-slice_bitcast_fusion.1, pred[512,256]{1,0:T(8,128)(4,1)S(1)} %broadcast_compare_fusion), kind=kOutput, calls=%fused_computation.10 | convolution fusion | flops 1090519040 | bytes 21692416 | tf_op jit(solution)/shard_map/while/body/eval_jaxpr/cond/branch_1_fun/hgij,ihgd->jhd/dot_general | solution.py:190
  403.1 37.8 %conditional.4 = ((f32[256,512]{0,1:T(8,128)S(1)}, f32[256,512]{0,1:T(8,128)S(1)})) conditional(s32[]{:T(128)} %convert_element_type.67, (f32[256,512]{0,1:T(8,128)S(1)}, f32[256,512]{0,1:T(8,128)S(1)}) %tuple.141, (s32[]{:T(128)}, bf16[2048,4096]{0,1:T(8,128)(2,1)}, s32[]{:T(128)}, s32[512]{0:T(512)S(1)}, bf16[256,4,128]{2,0,1:T(8,128)(2,1)S(1)}, ...), branch_computations={%region_12.12_spmd, %region_13.13_spmd} | conditional | flops 4337303552 | bytes 106239080 | solution.py:198
  411.7 8.1 %fusion.18 = f32[4,512,8,256]{3,1,2,0:T(8,128)} fusion(bf16[512,4,8,128]{0,3,2,1:T(8,128)(2,1)S(1)} %bitcast.220, bf16[256,4,128]{2,0,1:T(8,128)(2,1)S(1)} %get-tuple-element.449), kind=kOutput, calls=%fused_computation.16 | convolution fusion | flops 1073741824 | bytes 21233664 | tf_op jit(solution)/shard_map/while/body/eval_jaxpr/cond/branch_1_fun/ihgd,jhd->hgij/dot_general | solution.py:175
  419.8 11.8 %fusion.15 = f32[4,128,256,1]{2,1,3,0:T(8,128)S(1)} fusion(bf16[512,4,8,128]{0,3,2,1:T(8,128)(2,1)} %bitcast.221, f32[4,512,8,256]{3,1,2,0:T(8,128)} %fusion.18, bf16[512,4,8,128]{0,3,2,1:T(8,128)(2,1)} %bitcast.222, f32[4,8,512]{2,1,0:T(8,128)S(1)} %dynamic-slice_bitcast_fusion, f32[4,8,512]{2,1,0:T(8,128)S(1)} %dynamic-slice_bitcast_fusion.1, ...), kind=kOutput, calls=%fused_computation.12 | convolution fusion | flops 2172649472 | bytes 26214400 | tf_op jit(solution)/shard_map/while/body/eval_jaxpr/cond/branch_1_fun/hgij,ihgd->jhd/dot_general | solution.py:187
  431.6 9.1 %fusion.12 = f32[4,128,256,1]{2,1,3,0:T(8,128)S(1)} fusion(bf16[512,4,8,128]{0,3,2,1:T(8,128)(2,1)} %bitcast.223, f32[4,512,8,256]{3,1,2,0:T(8,128)} %fusion.18, f32[4,8,512]{2,1,0:T(8,128)S(1)} %dynamic-slice_bitcast_fusion.1, pred[512,256]{1,0:T(8,128)(4,1)S(1)} %broadcast_compare_fusion), kind=kOutput, calls=%fused_computation.10 | convolution fusion | flops 1090519040 | bytes 21692416 | tf_op jit(solution)/shard_map/while/body/eval_jaxpr/cond/branch_1_fun/hgij,ihgd->jhd/dot_general | solution.py:190
  442.2 37.8 %conditional.4 = ((f32[256,512]{0,1:T(8,128)S(1)}, f32[256,512]{0,1:T(8,128)S(1)})) conditional(s32[]{:T(128)} %convert_element_type.67, (f32[256,512]{0,1:T(8,128)S(1)}, f32[256,512]{0,1:T(8,128)S(1)}) %tuple.141, (s32[]{:T(128)}, bf16[2048,4096]{0,1:T(8,128)(2,1)}, s32[]{:T(128)}, s32[512]{0:T(512)S(1)}, bf16[256,4,128]{2,0,1:T(8,128)(2,1)S(1)}, ...), branch_computations={%region_12.12_spmd, %region_13.13_spmd} | conditional | flops 4337303552 | bytes 106239080 | solution.py:198
  450.9 8.1 %fusion.18 = f32[4,512,8,256]{3,1,2,0:T(8,128)} fusion(bf16[512,4,8,128]{0,3,2,1:T(8,128)(2,1)S(1)} %bitcast.220, bf16[256,4,128]{2,0,1:T(8,128)(2,1)S(1)} %get-tuple-element.449), kind=kOutput, calls=%fused_computation.16 | convolution fusion | flops 1073741824 | bytes 21233664 | tf_op jit(solution)/shard_map/while/body/eval_jaxpr/cond/branch_1_fun/ihgd,jhd->hgij/dot_general | solution.py:175
  459.0 11.8 %fusion.15 = f32[4,128,256,1]{2,1,3,0:T(8,128)S(1)} fusion(bf16[512,4,8,128]{0,3,2,1:T(8,128)(2,1)} %bitcast.221, f32[4,512,8,256]{3,1,2,0:T(8,128)} %fusion.18, bf16[512,4,8,128]{0,3,2,1:T(8,128)(2,1)} %bitcast.222, f32[4,8,512]{2,1,0:T(8,128)S(1)} %dynamic-slice_bitcast_fusion, f32[4,8,512]{2,1,0:T(8,128)S(1)} %dynamic-slice_bitcast_fusion.1, ...), kind=kOutput, calls=%fused_computation.12 | convolution fusion | flops 2172649472 | bytes 26214400 | tf_op jit(solution)/shard_map/while/body/eval_jaxpr/cond/branch_1_fun/hgij,ihgd->jhd/dot_general | solution.py:187
  470.8 9.1 %fusion.12 = f32[4,128,256,1]{2,1,3,0:T(8,128)S(1)} fusion(bf16[512,4,8,128]{0,3,2,1:T(8,128)(2,1)} %bitcast.223, f32[4,512,8,256]{3,1,2,0:T(8,128)} %fusion.18, f32[4,8,512]{2,1,0:T(8,128)S(1)} %dynamic-slice_bitcast_fusion.1, pred[512,256]{1,0:T(8,128)(4,1)S(1)} %broadcast_compare_fusion), kind=kOutput, calls=%fused_computation.10 | convolution fusion | flops 1090519040 | bytes 21692416 | tf_op jit(solution)/shard_map/while/body/eval_jaxpr/cond/branch_1_fun/hgij,ihgd->jhd/dot_general | solution.py:190
  481.4 37.8 %conditional.4 = ((f32[256,512]{0,1:T(8,128)S(1)}, f32[256,512]{0,1:T(8,128)S(1)})) conditional(s32[]{:T(128)} %convert_element_type.67, (f32[256,512]{0,1:T(8,128)S(1)}, f32[256,512]{0,1:T(8,128)S(1)}) %tuple.141, (s32[]{:T(128)}, bf16[2048,4096]{0,1:T(8,128)(2,1)}, s32[]{:T(128)}, s32[512]{0:T(512)S(1)}, bf16[256,4,128]{2,0,1:T(8,128)(2,1)S(1)}, ...), branch_computations={%region_12.12_spmd, %region_13.13_spmd} | conditional | flops 4337303552 | bytes 106239080 | solution.py:198
  498.2 11.8 %fusion.15 = f32[4,128,256,1]{2,1,3,0:T(8,128)S(1)} fusion(bf16[512,4,8,128]{0,3,2,1:T(8,128)(2,1)} %bitcast.221, f32[4,512,8,256]{3,1,2,0:T(8,128)} %fusion.18, bf16[512,4,8,128]{0,3,2,1:T(8,128)(2,1)} %bitcast.222, f32[4,8,512]{2,1,0:T(8,128)S(1)} %dynamic-slice_bitcast_fusion, f32[4,8,512]{2,1,0:T(8,128)S(1)} %dynamic-slice_bitcast_fusion.1, ...), kind=kOutput, calls=%fused_computation.12 | convolution fusion | flops 2172649472 | bytes 26214400 | tf_op jit(solution)/shard_map/while/body/eval_jaxpr/cond/branch_1_fun/hgij,ihgd->jhd/dot_general | solution.py:187
  510.0 9.1 %fusion.12 = f32[4,128,256,1]{2,1,3,0:T(8,128)S(1)} fusion(bf16[512,4,8,128]{0,3,2,1:T(8,128)(2,1)} %bitcast.223, f32[4,512,8,256]{3,1,2,0:T(8,128)} %fusion.18, f32[4,8,512]{2,1,0:T(8,128)S(1)} %dynamic-slice_bitcast_fusion.1, pred[512,256]{1,0:T(8,128)(4,1)S(1)} %broadcast_compare_fusion), kind=kOutput, calls=%fused_computation.10 | convolution fusion | flops 1090519040 | bytes 21692416 | tf_op jit(solution)/shard_map/while/body/eval_jaxpr/cond/branch_1_fun/hgij,ihgd->jhd/dot_general | solution.py:190
  (139 shorter events, 141.0 us)
Async XLA Ops:
  7.2 4.9 copy-start.3
  7.2 5.0 copy-start.4
  7.2 331.7 %all-gather.2.cloned.1.call-start = ((), (), s32[]{:S(2)}) async-start(), calls=%async_computation.1 | async-start | bytes 35651584 | tf_op jit(solution)/shard_map/all_gather | solution.py:18
  12.3 1.9 collective-permute-start
  14.4 4.4 copy-start.1
  18.8 144.1 %all-to-all-start = ((bf16[16,2,256,512]{3,2,1,0:T(8,128)(2,1)}), bf16[16,2,256,512]{3,2,1,0:T(8,128)(2,1)}, u32[]{:S(2)}, u32[]{:S(2)}) async-start(bf16[16,2,256,512]{3,2,1,0:T(8,128)(2,1)} %stack.14), calls=%async_computation | async-start | bytes 16777216 | tf_op jit(solution)/shard_map/all_to_all | solution.py:128
  338.9 23.6 %copy-start.2 = (bf16[256,4,128]{2,0,1:T(8,128)(2,1)S(1)}, bf16[256,4,128]{2,0,1:T(8,128)(2,1)}, u32[]{:S(2)}) copy-start(bf16[256,4,128]{2,0,1:T(8,128)(2,1)} %copy.97) | copy-start | bytes 786436
  366.6 5.9 %copy-start = (bf16[512,4096]{0,1:T(8,128)(2,1)}, bf16[512,4096]{0,1:T(8,128)(2,1)S(1)}, u32[]{:S(2)}) copy-start(bf16[512,4096]{0,1:T(8,128)(2,1)S(1)} %constant_dynamic-slice_fusion.1) | copy-start | bytes 12582916 | tf_op jit(solution)/shard_map/while/body/eval_jaxpr/cond
  405.8 5.9 %copy-start = (bf16[512,4096]{0,1:T(8,128)(2,1)}, bf16[512,4096]{0,1:T(8,128)(2,1)S(1)}, u32[]{:S(2)}) copy-start(bf16[512,4096]{0,1:T(8,128)(2,1)S(1)} %constant_dynamic-slice_fusion.1) | copy-start | bytes 12582916 | tf_op jit(solution)/shard_map/while/body/eval_jaxpr/cond
  444.9 5.9 %copy-start = (bf16[512,4096]{0,1:T(8,128)(2,1)}, bf16[512,4096]{0,1:T(8,128)(2,1)S(1)}, u32[]{:S(2)}) copy-start(bf16[512,4096]{0,1:T(8,128)(2,1)S(1)} %constant_dynamic-slice_fusion.1) | copy-start | bytes 12582916 | tf_op jit(solution)/shard_map/while/body/eval_jaxpr/cond
  484.1 5.9 %copy-start = (bf16[512,4096]{0,1:T(8,128)(2,1)}, bf16[512,4096]{0,1:T(8,128)(2,1)S(1)}, u32[]{:S(2)}) copy-start(bf16[512,4096]{0,1:T(8,128)(2,1)S(1)} %constant_dynamic-slice_fusion.1) | copy-start | bytes 12582916 | tf_op jit(solution)/shard_map/while/body/eval_jaxpr/cond
  520.4 7.6 %collective-permute-start.1 = (bf16[2,128,512]{2,1,0:T(8,128)(2,1)}, bf16[2,128,512]{2,1,0:T(8,128)(2,1)S(1)}, u32[]{:S(2)}, u32[]{:S(2)}) collective-permute-start(bf16[2,128,512]{2,1,0:T(8,128)(2,1)} %pad_maximum_fusion.2), channel_id=1, source_target_pairs={{0,1},{1,0},{2,3},{3,2},{4,5},{5,4},{6,7},{7,6},{8,9},{9,8},{10,11... | collective-permute-start | bytes 786440 | tf_op jit(solution)/shard_map/ppermute | solution.py:13
Sparse Core Ops, SparseCore 0:
  12.1 306.9 all-gather.1
